TPU v7x, 256 devices: a whole 4x4x8 slice. The times are simulated.
256 devices in a mesh: region: 16 (over z, x_hi), group: 16 (over y, x_lo, core).
Axes of the slice: x: 4 (x_hi: 2, x_lo: 2; x = x_hi * 2 + x_lo), y: 4, z: 8, core: 2. Of those that a mesh axis runs over, the one named last changes fastest.
Arguments:
- nodes: bfloat16 [65536, 512], P(('region', 'group')), may hold values from -6 to 6
- coarse: bfloat16 [512, 512], P(('region', 'group')), may hold values from -6 to 6
- edges: bfloat16 [393216, 512], P(('region', 'group')), may hold values from -6 to 6
- senders: int32 [393216], P(('region', 'group')), may hold values from 0 to 1279, as said below
- receivers: int32 [393216], P(('region', 'group')), may hold values from 0 to 127
- counts: int32 [512], P(('region', 'group')), may hold values from 96 to 768, as said below
- edge_in: bfloat16 [1536, 512], replicated, may hold values from -0.15625 to 0.15625
- edge_out: bfloat16 [512, 512], replicated, may hold values from -0.25 to 0.25
- edge_gain: float32 [512], replicated, may hold values from 0.1 to 1.9
- edge_shift: float32 [512], replicated, may hold values from -1.2 to 1.2
- node_in: bfloat16 [1024, 512], replicated, may hold values from -0.1875 to 0.1875
- node_out: bfloat16 [512, 512], replicated, may hold values from -0.25 to 0.25
- node_gain: float32 [512], replicated, may hold values from 0.1 to 1.9
- node_shift: float32 [512], replicated, may hold values from -3 to 3
Outputs:
- new_nodes: bfloat16 [65536, 512], P(('region', 'group'))
- new_coarse: bfloat16 [512, 512], P(('region', 'group'))
- new_edges: bfloat16 [393216, 512], P(('region', 'group'))
Inputs may be any that keep to these rules, and one draw needn't show every extreme that they name: `senders`: A sender below 256 never stands on a device of region 0, and one from 512 to 767 never on a device of the last region. `counts`: every device has a block with 768 live edges.
All inputs are finite; a program needn't handle non-finite values.
Results may differ from a plain program's by a relative error of at most 0.007.
Values may be sent and summed in bfloat16 or wider, within the bound.
No kernel may reach another device: no remote copies, remote signals or barrier semaphores. Data moves between devices by JAX's collectives and lax.ppermute only.
A program may use at most 64 MiB of HBM per device.

v0:
```python
import functools

import jax
import jax.numpy as jnp
from jax import lax
from jax.experimental import pallas as pl
from jax.experimental.pallas import tpu as pltpu
from jax.sharding import Mesh, PartitionSpec as P

F32 = jnp.float32
BF16 = jnp.bfloat16
LANES = 128
OWNED = 2
FINE = 768
STEP = 6
MIB = 1024 * 1024


def dot(a, b):
    return jnp.dot(a, b, preferred_element_type=F32)


def silu(x):
    half = 0.5 * x
    return half + half * jnp.tanh(half)


def normed(output, gain, shift):
    center = output - jnp.mean(output, axis=-1, keepdims=True)
    spread = jnp.mean(center * center, axis=-1, keepdims=True)
    return center * lax.rsqrt(spread + 1e-05) * gain + shift


def columns_of(ids_ref, first, count):
    parts = []
    for k in range(count):
        row = ids_ref[pl.ds(first + k, 1), :].astype(F32)
        parts.append(jnp.broadcast_to(row, (LANES, LANES)).T)
    return jnp.concatenate(parts, axis=0)


def rows_of(ids_ref, first, count):
    return jnp.concatenate([ids_ref[pl.ds(first + k, 1), :] for k in range(count)], axis=1)


def pick_rows(column, width, offset=0):
    lane = lax.broadcasted_iota(jnp.int32, column.shape, 1).astype(F32)
    parts = [
        (column == lane + float(offset + k * LANES)).astype(F32).astype(BF16)
        for k in range(width // LANES)
    ]
    return jnp.concatenate(parts, axis=1)


def local_kernel(
    core_ref,
    counts_ref,
    senders_ref,
    receivers_ref,
    edges_ref,
    nodes_ref,
    w_edge_ref,
    w_recv_ref,
    out_ref,
    places_ref,
    *,
    peers,
):
    block = pl.program_id(0)
    shape = places_ref.shape
    per_block = shape[0] // counts_ref.shape[0] * LANES
    row = lax.broadcasted_iota(jnp.int32, shape, 0)
    slot = row * LANES + lax.broadcasted_iota(jnp.int32, shape, 1)
    end = jnp.zeros(shape, jnp.int32)
    for b in range(counts_ref.shape[0]):
        end = jnp.where(slot >= b * per_block, b * per_block + counts_ref[b], end)
    ident = senders_ref[...] - FINE
    side = ((ident >> 1) & 1) ^ core_ref[0]
    place = (side * OWNED + (ident & 1)) * peers + (ident >> 2)
    places_ref[...] = jnp.where((slot < end) & (ident >= 0), place, -1)

    slots = edges_ref.shape[0]
    chunks = slots // LANES
    recv = columns_of(receivers_ref, block * chunks, chunks)
    offered = dot(nodes_ref[...], w_recv_ref[...]).astype(BF16)
    total = dot(edges_ref[...], w_edge_ref[...])
    total += dot(pick_rows(recv, nodes_ref.shape[0]), offered)
    out_ref[...] = total.astype(BF16)


def edge_update(before, sent, edges, w_mid_ref, w_out_ref, gain_ref, shift_ref):
    hidden = silu(before.astype(F32) + dot(sent, w_mid_ref[...])).astype(BF16)
    change = normed(dot(hidden, w_out_ref[...]), gain_ref[...], shift_ref[...])
    return (edges.astype(F32) + change).astype(BF16)


def fill(core_ref, table_ref, spread_rows, table):
    half = table.shape[0] // 2
    peers = half // OWNED
    spread_rows[: table_ref.shape[0], :] = table_ref[...].astype(F32)

    def from_core(core):
        for side in range(2):
            for r in range(8):
                q, j = r // OWNED, r % OWNED
                first = side * half + j * peers
                table[first : first + peers, q * LANES : (q + 1) * LANES] = spread_rows[
                    pl.ds((side ^ core) * 8 * peers + r, peers, stride=8), :
                ].astype(BF16)

    for core in range(2):
        pl.when(core_ref[0] == core)(functools.partial(from_core, core))


def coarse_edge_kernel(
    core_ref,
    places,
    before_ref,
    edges_ref,
    table_ref,
    w_in_ref,
    w_out_ref,
    gain_ref,
    shift_ref,
    to_mine_ref,
    to_other_ref,
    edges,
    w_mid,
    w_out,
    table,
    spread_rows,
    updated,
    sent,
    sems,
):
    slot_count, latent = edges.shape
    chunks = slot_count // LANES
    half = table.shape[0] // 2
    peers = half // OWNED
    tiles = chunks // STEP
    tile = STEP * LANES

    def copy(src, dst, k):
        one = pltpu.make_async_copy(src, dst, sems.at[k])
        one.start()
        return one

    weights = copy(w_in_ref.at[pl.ds(latent, latent), :], w_mid, 2)
    inputs = []
    for t in range(tiles):
        rows = pl.ds(t * tile, tile)
        inputs.append(
            [
                copy(edges_ref.at[rows, :], edges.at[rows, :], 5 + 3 * t),
            ]
        )
        if t == 0:
            weights_out = copy(w_out_ref, w_out, 3)
    fill(core_ref, table_ref, spread_rows, table)
    for t in range(tiles):
        rows = slice(t * tile, (t + 1) * tile)
        column = columns_of(places, t * STEP, STEP)
        sent[rows, :] = dot(pick_rows(column, 2 * half), table[...]).astype(BF16)
    weights.wait()
    for t in range(tiles):
        for one in inputs[t]:
            one.wait()
        if t == 0:
            weights_out.wait()
        rows = slice(t * tile, (t + 1) * tile)
        updated[rows, :] = edge_update(
            before_ref[rows, :], sent[rows, :], edges[rows, :], w_mid, w_out, gain_ref, shift_ref
        )
    row = rows_of(places, 0, chunks)
    target = lax.broadcasted_iota(jnp.int32, (2 * half, slot_count), 0)
    total = dot((row == target).astype(F32).astype(BF16), updated[...])
    for i, ref in enumerate((to_mine_ref, to_other_ref)):
        for r in range(8):
            q, j = r // OWNED, r % OWNED
            first = i * half + j * peers
            spread_rows[pl.ds(r, peers, stride=8), :] = total[
                first : first + peers, q * LANES : (q + 1) * LANES
            ]
        ref[...] = spread_rows[: half * latent // LANES, :].astype(BF16)


def fine_edge_kernel(
    core_ref,
    counts_ref,
    places_ref,
    senders_ref,
    receivers_ref,
    before_ref,
    edges_ref,
    table_ref,
    low_ref,
    nodes_ref,
    high_ref,
    w_mid_ref,
    w_out_ref,
    gain_ref,
    shift_ref,
    node_in_ref,
    node_out_ref,
    node_gain_ref,
    node_shift_ref,
    new_edges_ref,
    new_nodes_ref,
    spread_rows,
    table,
):
    block = pl.program_id(0)
    slots, latent = edges_ref.shape
    node_rows = nodes_ref.shape[0]
    block_size = new_nodes_ref.shape[0]
    chunks = slots // LANES

    @pl.when(block == 0)
    def _():
        fill(core_ref, table_ref, spread_rows, table)

    fresh = []
    for k in range(0, chunks, STEP):
        rows = slice(k * LANES, (k + STEP) * LANES)
        column = columns_of(senders_ref, block * chunks + k, STEP)
        place = columns_of(places_ref, block * chunks + k, STEP)
        sent = (
            dot(pick_rows(place, table.shape[0]), table[...])
            + dot(pick_rows(column, node_rows), low_ref[...])
            + dot(pick_rows(column, node_rows, node_rows), nodes_ref[...])
            + dot(pick_rows(column, node_rows, 2 * node_rows), high_ref[...])
        ).astype(BF16)
        old = edges_ref[rows, :]
        new = edge_update(
            before_ref[rows, :], sent, old, w_mid_ref, w_out_ref, gain_ref, shift_ref
        )
        slot = lax.broadcasted_iota(jnp.int32, (STEP * LANES, 1), 0) + k * LANES
        new = jnp.where(slot < counts_ref[block], new, old)
        new_edges_ref[rows, :] = new
        fresh.append(new)
    row = rows_of(receivers_ref, block * chunks, chunks)
    slot = lax.broadcasted_iota(jnp.int32, (1, slots), 1)
    row = jnp.where(slot < counts_ref[block], row, -1)
    target = lax.broadcasted_iota(jnp.int32, (block_size, slots), 0)
    pick = (row == target).astype(F32).astype(BF16)
    fine_sum = dot(pick, jnp.concatenate(fresh, axis=0)).astype(BF16)
    nodes = nodes_ref[pl.ds(pl.multiple_of(block * block_size, block_size), block_size), :]
    hidden = silu(dot(nodes, node_in_ref[:latent, :]) + dot(fine_sum, node_in_ref[latent:, :]))
    change = normed(
        dot(hidden.astype(BF16), node_out_ref[...]), node_gain_ref[...], node_shift_ref[...]
    )
    new_nodes_ref[...] = (nodes.astype(F32) + change).astype(BF16)


def coarse_kernel(
    parts_ref,
    coarse_ref,
    w_in_ref,
    w_out_ref,
    gain_ref,
    shift_ref,
    out_ref,
    rows,
    joined,
):
    owned, latent = coarse_ref.shape
    quarters = latent // LANES
    rows[...] = jnp.sum(parts_ref[...].astype(F32), axis=0)
    joined[...] = jnp.zeros(joined.shape, F32)
    coarse = coarse_ref[...].astype(F32)
    joined[:owned, :latent] = coarse
    for q in range(quarters):
        joined[:owned, latent + q * LANES : latent + (q + 1) * LANES] = rows[
            q * owned : (q + 1) * owned, :
        ]
    hidden = silu(dot(joined[...].astype(BF16), w_in_ref[...])).astype(BF16)
    change = normed(dot(hidden, w_out_ref[...]), gain_ref[...], shift_ref[...])
    out_ref[...] = (coarse + change[:owned, :]).astype(BF16)


def whole(shape):
    return pl.BlockSpec(shape, lambda *_: (0,) * len(shape))


def in_hbm(*arrays):
    return [pltpu.with_memory_space_constraint(a, pltpu.HBM) for a in arrays]


def coarse_edges(
    core, places, before, edges, table, edge_in, edge_out, gain, shift
):
    slot_count, latent = edges.shape
    flat = jax.ShapeDtypeStruct((table.shape[0] // 2, LANES), BF16)
    half = flat.shape[0] * flat.shape[1] // latent
    tiles = slot_count // (STEP * LANES)
    smem = pl.BlockSpec(memory_space=pltpu.SMEM)
    vmem, anywhere = pl.BlockSpec(memory_space=pltpu.VMEM), pl.BlockSpec(memory_space=pl.ANY)
    edges, edge_in, edge_out = in_hbm(edges, edge_in, edge_out)
    return pl.pallas_call(
        coarse_edge_kernel,
        in_specs=[smem, vmem, vmem, anywhere, vmem, anywhere, anywhere, vmem, vmem],
        out_specs=[vmem, vmem],
        out_shape=[flat, flat],
        scratch_shapes=[
            pltpu.VMEM(edges.shape, BF16),
            pltpu.VMEM((latent, latent), BF16),
            pltpu.VMEM((latent, latent), BF16),
            pltpu.VMEM((2 * half, latent), BF16),
            pltpu.VMEM((table.shape[0] + 8, LANES), F32),
            pltpu.VMEM(edges.shape, BF16),
            pltpu.VMEM(edges.shape, BF16),
            pltpu.SemaphoreType.DMA((4 + 3 * tiles,)),
        ],
        compiler_params=pltpu.CompilerParams(vmem_limit_bytes=40 * MIB),
        cost_estimate=pl.CostEstimate(flops=0, bytes_accessed=0, transcendentals=0),
        name="coarse_edges",
    )(core, places, before, edges, table, edge_in, edge_out, gain, shift)


def on_device(
    nodes,
    coarse,
    edges,
    senders,
    receivers,
    counts,
    edge_in,
    edge_out,
    edge_gain,
    edge_shift,
    node_in,
    node_out,
    node_gain,
    node_shift,
):
    node_rows, latent = nodes.shape
    owned = coarse.shape[0]
    blocks = counts.shape[0]
    slot_count = edges.shape[0]
    slots = slot_count // blocks
    regions = lax.axis_size("region")
    peers = regions * lax.axis_size("pair")
    core = lax.axis_index("core")
    smem = pl.BlockSpec(memory_space=pltpu.SMEM)
    gain_e, shift_e = edge_gain.reshape(1, latent), edge_shift.reshape(1, latent)
    gain_n, shift_n = node_gain.reshape(1, latent), node_shift.reshape(1, latent)
    swap = [(0, 1), (1, 0)]

    chunk = (owned * latent // LANES, LANES)
    small = coarse.reshape(owned, latent // LANES, LANES).transpose(1, 0, 2)
    copies = jnp.broadcast_to(small.reshape(1, *chunk), (peers,) + chunk)
    table = lax.all_to_all(copies, ("region", "pair"), 0, 0, tiled=True)

    forward = [(i, (i + 1) % regions) for i in range(regions)]
    backward = [((i + 1) % regions, i) for i in range(regions)]
    low = lax.ppermute(nodes, "region", forward)
    high = lax.ppermute(nodes, "region", backward)

    send_grid = senders.reshape(-1, LANES)
    recv_grid = receivers.reshape(-1, LANES)
    row_block = pl.BlockSpec((slots, latent), lambda b: (b, 0))
    node_block = pl.BlockSpec((node_rows // blocks, latent), lambda b: (b, 0))

    def w_part(k):
        return pl.BlockSpec((latent, latent), lambda b: (k, 0))

    core = core.reshape(1)
    before, places = pl.pallas_call(
        functools.partial(local_kernel, peers=peers),
        grid=(blocks,),
        in_specs=[smem, smem, whole(send_grid.shape), whole(recv_grid.shape), row_block, node_block, w_part(0), w_part(2)],
        out_specs=[row_block, whole(send_grid.shape)],
        out_shape=[
            pltpu.VMEM((slot_count, latent), BF16),
            pltpu.VMEM(send_grid.shape, jnp.int32),
        ],
        compiler_params=pltpu.CompilerParams(vmem_limit_bytes=60 * MIB),
        cost_estimate=pl.CostEstimate(
            flops=2 * slot_count * latent * (2 * latent + LANES),
            bytes_accessed=6 * MIB,
            transcendentals=0,
        ),
        name="local",
    )(core, counts, send_grid, recv_grid, *in_hbm(edges, nodes, edge_in, edge_in))

    table, before = lax.optimization_barrier((table, before))
    table = lax.all_gather(table.reshape(-1, LANES), "core", axis=0, tiled=True)
    to_mine, to_other = coarse_edges(
        core, places, before, edges, table, edge_in, edge_out, gain_e, shift_e
    )
    to_other, low, high = lax.optimization_barrier((to_other, low, high))
    arrived = lax.ppermute(to_other, "core", swap)
    chip_sum = (to_mine.astype(F32) + arrived.astype(F32)).astype(BF16)
    chip_sum, before = lax.optimization_barrier((chip_sum, before))
    parts = lax.all_to_all(
        chip_sum.reshape((peers,) + chunk), ("region", "pair"), 0, 0, tiled=True
    )

    new_edges, new_nodes = pl.pallas_call(
        fine_edge_kernel,
        grid=(blocks,),
        in_specs=[
            smem,
            smem,
            whole(send_grid.shape),
            whole(send_grid.shape),
            whole(recv_grid.shape),
            row_block,
            row_block,
            whole(table.shape),
            whole(nodes.shape),
            whole(nodes.shape),
            whole(nodes.shape),
            w_part(1),
            whole(edge_out.shape),
            whole(gain_e.shape),
            whole(gain_e.shape),
            whole(node_in.shape),
            whole(node_out.shape),
            whole(gain_n.shape),
            whole(gain_n.shape),
        ],
        out_specs=[row_block, node_block],
        out_shape=[
            jax.ShapeDtypeStruct(edges.shape, BF16),
            jax.ShapeDtypeStruct(nodes.shape, BF16),
        ],
        scratch_shapes=[
            pltpu.VMEM((table.shape[0] + 8, LANES), F32),
            pltpu.VMEM((2 * peers * owned, latent), BF16),
        ],
        compiler_params=pltpu.CompilerParams(vmem_limit_bytes=60 * MIB),
        cost_estimate=pl.CostEstimate(
            flops=2 * slot_count * latent * (4 * latent + 2 * LANES),
            bytes_accessed=10 * MIB,
            transcendentals=slot_count * latent,
        ),
        name="fine_edges",
    )(
        core,
        counts,
        places,
        send_grid,
        recv_grid,
        before,
        edges,
        table,
        low,
        nodes,
        high,
        edge_in,
        edge_out,
        gain_e,
        shift_e,
        node_in,
        node_out,
        gain_n,
        shift_n,
    )

    new_coarse = pl.pallas_call(
        coarse_kernel,
        in_specs=[pl.BlockSpec(memory_space=pltpu.VMEM)] * 6,
        out_specs=pl.BlockSpec(memory_space=pltpu.VMEM),
        out_shape=jax.ShapeDtypeStruct(coarse.shape, BF16),
        scratch_shapes=[pltpu.VMEM(chunk, F32), pltpu.VMEM((8, 2 * latent), F32)],
        compiler_params=pltpu.CompilerParams(vmem_limit_bytes=16 * MIB),
        name="coarse_nodes",
    )(parts, coarse, node_in, node_out, gain_n, shift_n)
    return (new_nodes, new_coarse, new_edges)


def solution(mesh):
    regions, groups = mesh.devices.shape
    fine = Mesh(mesh.devices.reshape(regions, groups // 2, 2), ("region", "pair", "core"))
    every = ("region", "pair", "core")
    rows, flat, copied = P(every, None), P(every), P()
    return jax.shard_map(
        on_device,
        mesh=fine,
        in_specs=(rows, rows, rows, flat, flat, flat) + (copied,) * 8,
        out_specs=(rows, rows, rows),
        check_vma=False,
    )
```

profile of v0, /device:TPU:32, one launch (start us, length us, event | category | flops | bytes accessed | tf_op | source)
XLA Modules:
  0.0 65.2 jit_solution(12665340832667524756)
XLA Ops:
  0.6 1.4 %broadcast_in_dim.8 = bf16[128,8,128]{2,1,0:T(8,128)(2,1)} broadcast(bf16[8,128]{1,0:T(8,128)(2,1)} %bitcast.14), dimensions={1,2} | broadcast | bytes 264192 | tf_op jit(solution)/shard_map/broadcast_in_dim | solution.py:351
  2.0 15.0 %all-to-all-start = ((bf16[128,8,128]{2,1,0:T(8,128)(2,1)}), bf16[128,8,128]{2,1,0:T(8,128)(2,1)S(1)}, u32[]{:S(2)}, u32[]{:S(2)}) async-start(bf16[128,8,128]{2,1,0:T(8,128)(2,1)} %broadcast_in_dim.8), calls=%async_computation | async-start | bytes 524288 | tf_op jit(solution)/shard_map/all_to_all | solution.py:352
  17.1 3.1 %collective-permute-start = (bf16[256,512]{1,0:T(8,128)(2,1)}, bf16[256,512]{1,0:T(8,128)(2,1)S(1)}, u32[]{:S(2)}, u32[]{:S(2)}) collective-permute-start(bf16[256,512]{1,0:T(8,128)(2,1)} %nodes_ref.3), channel_id=1, source_target_pairs={{0,16},{16,32},{32,48},{48,64},{64,80},{80,96},{96,112},{112,128},... | collective-permute-start | bytes 786440 | tf_op jit(solution)/shard_map/ppermute | solution.py:356
  20.1 1.4 %collective-permute-start.1 = (bf16[256,512]{1,0:T(8,128)(2,1)}, bf16[256,512]{1,0:T(8,128)(2,1)S(1)}, u32[]{:S(2)}, u32[]{:S(2)}) collective-permute-start(bf16[256,512]{1,0:T(8,128)(2,1)} %nodes_ref.3), channel_id=1, source_target_pairs={{16,0},{32,16},{48,32},{64,48},{80,64},{96,80},{112,96},{128,112},... | collective-permute-start | bytes 786440 | tf_op jit(solution)/shard_map/ppermute | solution.py:357
  21.6 3.6 %local.1 = (bf16[1536,512]{1,0:T(8,128)(2,1)S(1)}, s32[12,128]{1,0:T(8,128)S(1)}) custom-call(s32[1]{0:T(128)} %bitcast.core_ref, s32[2]{0:T(128)} %counts_ref.3, s32[12,128]{1,0:T(8,128)} %bitcast.24, s32[12,128]{1,0:T(8,128)} %bitcast.26, bf16[1536,512]{1,0:T(8,128)(2,1)} %edges_ref.5, bf16[256,512]{1,0:T(8,128)(2,1)} %nodes_ref.3, ...), custom_call_target="tpu_custom_call" | custom-call | flops 1811939328 | bytes 6291456 | tf_op jit(solution)/shard_map/local/pallas_call | solution.py:368
  25.1 0.0 copy-start.1
  25.2 0.0 copy-start.4
  25.2 6.5 %all-to-all-done = bf16[128,8,128]{2,1,0:T(8,128)(2,1)S(1)} async-done(((bf16[128,8,128]{2,1,0:T(8,128)(2,1)}), bf16[128,8,128]{2,1,0:T(8,128)(2,1)S(1)}, u32[]{:S(2)}, u32[]{:S(2)}) %all-to-all-start) | async-done | bytes 262176 | tf_op jit(solution)/shard_map/all_to_all | solution.py:352
  31.7 2.2 %all_gather.3.table_ref = bf16[2048,128]{1,0:T(8,128)(2,1)S(1)} all-gather(bf16[1024,128]{1,0:T(8,128)(2,1)S(1)} %bitcast.23), channel_id=1, replica_groups=mesh['region'=16,'pair'=8,'core'=2] {'core'}, dimensions={0}, use_global_device_ids=true | all-gather | bytes 786432 | tf_op jit(solution)/shard_map/all_gather | solution.py:387
  33.8 0.0 copy-done.6
  33.8 0.0 copy-done.7
  33.8 5.6 %coarse_edges.1 = (bf16[1024,128]{1,0:T(8,128)(2,1)S(1)}, bf16[1024,128]{1,0:T(8,128)(2,1)S(1)}) custom-call(s32[1]{0:T(128)} %bitcast.core_ref, s32[12,128]{1,0:T(8,128)S(1)} %get-tuple-element.16.places.places_ref, bf16[1536,512]{1,0:T(8,128)(2,1)S(1)} %get-tuple-element.23.before_ref, bf16[1536,512]{1,0:T(8,128)(2,1)} %edges_ref.5, ...), custom_call_target="tpu_custom_call" | custom-call | tf_op jit(solution)/shard_map/coarse_edges/pallas_call | solution.py:299
  39.5 0.0 copy-done.1
  39.5 0.0 copy-done.4
  39.5 0.0 copy-done
  39.5 0.0 collective-permute-done.low_ref
  39.5 0.0 copy-start.10
  39.5 0.0 collective-permute-done.1.high_ref
  39.5 0.2 collective-permute-start.2
  39.8 1.4 %collective-permute-done.2 = bf16[1024,128]{1,0:T(8,128)(2,1)S(1)} collective-permute-done((bf16[1024,128]{1,0:T(8,128)(2,1)S(1)}, bf16[1024,128]{1,0:T(8,128)(2,1)S(1)}, u32[]{:S(2)}, u32[]{:S(2)}) %collective-permute-start.2) | collective-permute-done | bytes 262176 | tf_op jit(solution)/shard_map/ppermute | solution.py:392
  41.2 0.8 %add_convert_fusion = bf16[1024,128]{1,0:T(8,128)(2,1)} fusion(bf16[1024,128]{1,0:T(8,128)(2,1)S(1)} %collective-permute-done.2, bf16[1024,128]{1,0:T(8,128)(2,1)S(1)} %get-tuple-element.20), kind=kLoop, calls=%fused_computation | loop fusion | flops 524288 | bytes 786432 | tf_op jit(solution)/shard_map/convert_element_type | solution.py:393
  42.0 7.1 %all-to-all-start.1 = ((bf16[128,8,128]{2,1,0:T(8,128)(2,1)}), bf16[128,8,128]{2,1,0:T(8,128)(2,1)S(1)}, u32[]{:S(2)}, u32[]{:S(2)}) async-start(bf16[128,8,128]{2,1,0:T(8,128)(2,1)} %bitcast.11), calls=%async_computation.1 | async-start | bytes 524288 | tf_op jit(solution)/shard_map/all_to_all | solution.py:395
  49.1 0.0 copy-start.2
  49.1 0.0 copy-start.3
  49.1 0.0 copy-start.5
  49.1 0.0 copy-start.8
  49.1 0.0 copy-start.9
  49.1 11.0 %fine_edges.1 = (bf16[1536,512]{1,0:T(8,128)(2,1)}, bf16[256,512]{1,0:T(8,128)(2,1)}) custom-call(s32[1]{0:T(128)} %bitcast.core_ref, s32[2]{0:T(128)} %counts_ref.3, s32[12,128]{1,0:T(8,128)} %copy-done.4, s32[12,128]{1,0:T(8,128)} %bitcast.25, s32[12,128]{1,0:T(8,128)} %bitcast.27, bf16[1536,512]{1,0:T(8,128)(2,1)} %copy-done.1, ...), custom_call_target="tpu_custom_call" | custom-call | flops 3623878656 | bytes 10485760 | tf_op jit(solution)/shard_map/fine_edges/pallas_call | solution.py:399
  60.2 3.7 %all-to-all-done.1.parts_ref = bf16[128,8,128]{2,1,0:T(8,128)(2,1)S(1)} async-done(((bf16[128,8,128]{2,1,0:T(8,128)(2,1)}), bf16[128,8,128]{2,1,0:T(8,128)(2,1)S(1)}, u32[]{:S(2)}, u32[]{:S(2)}) %all-to-all-start.1) | async-done | bytes 262176 | tf_op jit(solution)/shard_map/all_to_all | solution.py:395
  63.9 0.0 copy-done.8
  63.9 0.0 copy-done.9
  63.9 1.3 %coarse_nodes.1 = bf16[2,512]{1,0:T(2,128)(2,1)} custom-call(bf16[128,8,128]{2,1,0:T(8,128)(2,1)S(1)} %all-to-all-done.1.parts_ref, bf16[2,512]{1,0:T(2,128)(2,1)S(1)} %copy-done.5, bf16[1024,512]{1,0:T(8,128)(2,1)S(1)} %copy-done.2, bf16[512,512]{1,0:T(8,128)(2,1)S(1)} %copy-done.3, f32[1,512]{1,0:T(1,128)S(1)} %bitcast.20, f32[1,512]{1,0:T(1,128)S(1)} %bitcast.22), custom_call_target="tpu_custom_call" | custom-call | tf_op jit(solution)/shard_map/coarse_nodes/pallas_call | solution.py:461
  (9 shorter events, 0.0 us)
Async XLA Ops:
  2.0 29.6 %all-to-all-start = ((bf16[128,8,128]{2,1,0:T(8,128)(2,1)}), bf16[128,8,128]{2,1,0:T(8,128)(2,1)S(1)}, u32[]{:S(2)}, u32[]{:S(2)}) async-start(bf16[128,8,128]{2,1,0:T(8,128)(2,1)} %broadcast_in_dim.8), calls=%async_computation | async-start | bytes 524288 | tf_op jit(solution)/shard_map/all_to_all | solution.py:352
  17.1 22.4 %collective-permute-start = (bf16[256,512]{1,0:T(8,128)(2,1)}, bf16[256,512]{1,0:T(8,128)(2,1)S(1)}, u32[]{:S(2)}, u32[]{:S(2)}) collective-permute-start(bf16[256,512]{1,0:T(8,128)(2,1)} %nodes_ref.3), channel_id=1, source_target_pairs={{0,16},{16,32},{32,48},{48,64},{64,80},{80,96},{96,112},{112,128},... | collective-permute-start | bytes 786440 | tf_op jit(solution)/shard_map/ppermute | solution.py:356
  20.1 19.4 %collective-permute-start.1 = (bf16[256,512]{1,0:T(8,128)(2,1)}, bf16[256,512]{1,0:T(8,128)(2,1)S(1)}, u32[]{:S(2)}, u32[]{:S(2)}) collective-permute-start(bf16[256,512]{1,0:T(8,128)(2,1)} %nodes_ref.3), channel_id=1, source_target_pairs={{16,0},{32,16},{48,32},{64,48},{80,64},{96,80},{112,96},{128,112},... | collective-permute-start | bytes 786440 | tf_op jit(solution)/shard_map/ppermute | solution.py:357
  21.6 12.3 %copy-start.6 = (f32[512]{0:T(512)S(1)}, f32[512]{0:T(512)}, u32[]{:S(2)}) copy-start(f32[512]{0:T(512)} %param.22) | copy-start | bytes 6148
  21.6 12.3 %copy-start.7 = (f32[512]{0:T(512)S(1)}, f32[512]{0:T(512)}, u32[]{:S(2)}) copy-start(f32[512]{0:T(512)} %param.23) | copy-start | bytes 6148
  25.1 14.3 %copy-start.1 = (bf16[1536,512]{1,0:T(8,128)(2,1)}, bf16[1536,512]{1,0:T(8,128)(2,1)S(1)}, u32[]{:S(2)}) copy-start(bf16[1536,512]{1,0:T(8,128)(2,1)S(1)} %get-tuple-element.23.before_ref) | copy-start | bytes 4718596
  25.2 14.3 %copy-start.4 = (s32[12,128]{1,0:T(8,128)}, s32[12,128]{1,0:T(8,128)S(1)}, u32[]{:S(2)}) copy-start(s32[12,128]{1,0:T(8,128)S(1)} %get-tuple-element.16.places.places_ref) | copy-start | bytes 18436
  33.8 5.7 %copy-start = (bf16[2048,128]{1,0:T(8,128)(2,1)}, bf16[2048,128]{1,0:T(8,128)(2,1)S(1)}, u32[]{:S(2)}) copy-start(bf16[2048,128]{1,0:T(8,128)(2,1)S(1)} %all_gather.3.table_ref) | copy-start | bytes 1572868
  39.5 9.5 %copy-start.10 = (bf16[256,512]{1,0:T(8,128)(2,1)}, bf16[256,512]{1,0:T(8,128)(2,1)S(1)}, u32[]{:S(2)}) copy-start(bf16[256,512]{1,0:T(8,128)(2,1)S(1)} %collective-permute-done.low_ref) | copy-start | bytes 786436
  39.5 9.5 %copy-start.11 = (bf16[256,512]{1,0:T(8,128)(2,1)}, bf16[256,512]{1,0:T(8,128)(2,1)S(1)}, u32[]{:S(2)}) copy-start(bf16[256,512]{1,0:T(8,128)(2,1)S(1)} %collective-permute-done.1.high_ref) | copy-start | bytes 786436
  39.5 1.6 %collective-permute-start.2 = (bf16[1024,128]{1,0:T(8,128)(2,1)S(1)}, bf16[1024,128]{1,0:T(8,128)(2,1)S(1)}, u32[]{:S(2)}, u32[]{:S(2)}) collective-permute-start(bf16[1024,128]{1,0:T(8,128)(2,1)S(1)} %get-tuple-element.22), channel_id=1, source_target_pairs={{0,1},{1,0},{2,3},{3,2},{4,5},{5,4},{6,7},{7,6},{8,9},{9,8},{10,11... | collective-permute-start | bytes 786440 | tf_op jit(solution)/shard_map/ppermute | solution.py:392
  42.0 21.9 %all-to-all-start.1 = ((bf16[128,8,128]{2,1,0:T(8,128)(2,1)}), bf16[128,8,128]{2,1,0:T(8,128)(2,1)S(1)}, u32[]{:S(2)}, u32[]{:S(2)}) async-start(bf16[128,8,128]{2,1,0:T(8,128)(2,1)} %bitcast.11), calls=%async_computation.1 | async-start | bytes 524288 | tf_op jit(solution)/shard_map/all_to_all | solution.py:395
  49.1 14.8 %copy-start.2 = (bf16[1024,512]{1,0:T(8,128)(2,1)S(1)}, bf16[1024,512]{1,0:T(8,128)(2,1)}, u32[]{:S(2)}) copy-start(bf16[1024,512]{1,0:T(8,128)(2,1)} %w_in_ref.3) | copy-start | bytes 3145732
  49.1 14.8 %copy-start.3 = (bf16[512,512]{1,0:T(8,128)(2,1)S(1)}, bf16[512,512]{1,0:T(8,128)(2,1)}, u32[]{:S(2)}) copy-start(bf16[512,512]{1,0:T(8,128)(2,1)} %w_out_ref.5) | copy-start | bytes 1572868
  49.1 14.8 %copy-start.5 = (bf16[2,512]{1,0:T(2,128)(2,1)S(1)}, bf16[2,512]{1,0:T(2,128)(2,1)}, u32[]{:S(2)}) copy-start(bf16[2,512]{1,0:T(2,128)(2,1)} %coarse_ref.1) | copy-start | bytes 6148
  49.1 14.8 %copy-start.8 = (f32[512]{0:T(512)S(1)}, f32[512]{0:T(512)}, u32[]{:S(2)}) copy-start(f32[512]{0:T(512)} %param.26) | copy-start | bytes 6148
  49.1 14.8 %copy-start.9 = (f32[512]{0:T(512)S(1)}, f32[512]{0:T(512)}, u32[]{:S(2)}) copy-start(f32[512]{0:T(512)} %param.27) | copy-start | bytes 6148
where the time goes:
time: 65.5 us; the launch traced here: 65.2 us
  starting transfers between devices  26.8 us (41%)
  Pallas kernels  21.5 us (33%)
  waiting for transfers between devices  11.6 us (18%)
  blocking collectives  2.17 us (3%)
  local copies, waits for them, and re-layouts  1.48 us (2%)
  between operations  0.82 us (1%)
  other arithmetic  0.78 us (1%)
    all_to_all x1, starting transfers between devices, on_device(): table = lax.all_to_all(copies, ('region', 'pair'), 0, 0, tiled=True)  15 us
    pallas_call x1, Pallas kernels, on_device(): pl.pallas_call(fine_edge_kernel, grid=(blocks,), in_specs=[smem, smem, wh...  11 us
    all_to_all x1, starting transfers between devices, on_device(): lax.all_to_all(chip_sum.reshape((peers,) + chunk), ('region', 'pair'), 0,...  7.09 us
    all_to_all x1, waiting for transfers between devices, on_device(): table = lax.all_to_all(copies, ('region', 'pair'), 0, 0, tiled=True)  6.49 us
    pallas_call x1, Pallas kernels, coarse_edges(): pl.pallas_call(coarse_edge_kernel, in_specs=[smem, vmem, vmem, anywhere,...  5.63 us
    all_to_all x1, waiting for transfers between devices, on_device(): lax.all_to_all(chip_sum.reshape((peers,) + chunk), ('region', 'pair'), 0,...  3.72 us
    pallas_call x1, Pallas kernels, on_device(): pl.pallas_call(functools.partial(local_kernel, peers=peers), grid=(blocks...  3.56 us
    ppermute x1, starting transfers between devices, on_device(): low = lax.ppermute(nodes, 'region', forward)  3.08 us
  transfers between devices with their start and end apart: 5, of which 3 were waited for; matrix products, arithmetic and copies ran while one was open for 0% of the time, Pallas kernels for 31%

commit v1 on v0

--- a/solution.py
+++ b/solution.py
@@ -200,14 +200,17 @@
     w_out_ref,
     gain_ref,
     shift_ref,
+    coarse_ref,
     node_in_ref,
     node_out_ref,
     node_gain_ref,
     node_shift_ref,
     new_edges_ref,
     new_nodes_ref,
+    begun_ref,
     spread_rows,
     table,
+    padded,
 ):
     block = pl.program_id(0)
     slots, latent = edges_ref.shape
@@ -218,6 +221,9 @@
     @pl.when(block == 0)
     def _():
         fill(core_ref, table_ref, spread_rows, table)
+        padded[...] = jnp.zeros(padded.shape, F32)
+        padded[: coarse_ref.shape[0], :] = coarse_ref[...].astype(F32)
+        begun_ref[...] = dot(padded[...].astype(BF16), node_in_ref[:latent, :])
 
     fresh = []
     for k in range(0, chunks, STEP):
@@ -255,6 +261,7 @@
 def coarse_kernel(
     parts_ref,
     coarse_ref,
+    begun_ref,
     w_in_ref,
     w_out_ref,
     gain_ref,
@@ -268,12 +275,11 @@
     rows[...] = jnp.sum(parts_ref[...].astype(F32), axis=0)
     joined[...] = jnp.zeros(joined.shape, F32)
     coarse = coarse_ref[...].astype(F32)
-    joined[:owned, :latent] = coarse
     for q in range(quarters):
-        joined[:owned, latent + q * LANES : latent + (q + 1) * LANES] = rows[
+        joined[:owned, q * LANES : (q + 1) * LANES] = rows[
             q * owned : (q + 1) * owned, :
         ]
-    hidden = silu(dot(joined[...].astype(BF16), w_in_ref[...])).astype(BF16)
+    hidden = silu(begun_ref[...] + dot(joined[...].astype(BF16), w_in_ref[latent:, :])).astype(BF16)
     change = normed(dot(hidden, w_out_ref[...]), gain_ref[...], shift_ref[...])
     out_ref[...] = (coarse + change[:owned, :]).astype(BF16)
 
@@ -396,7 +402,7 @@
         chip_sum.reshape((peers,) + chunk), ("region", "pair"), 0, 0, tiled=True
     )
 
-    new_edges, new_nodes = pl.pallas_call(
+    new_edges, new_nodes, begun = pl.pallas_call(
         fine_edge_kernel,
         grid=(blocks,),
         in_specs=[
@@ -415,19 +421,22 @@
             whole(edge_out.shape),
             whole(gain_e.shape),
             whole(gain_e.shape),
+            whole(coarse.shape),
             whole(node_in.shape),
             whole(node_out.shape),
             whole(gain_n.shape),
             whole(gain_n.shape),
         ],
-        out_specs=[row_block, node_block],
+        out_specs=[row_block, node_block, whole((8, latent))],
         out_shape=[
             jax.ShapeDtypeStruct(edges.shape, BF16),
             jax.ShapeDtypeStruct(nodes.shape, BF16),
+            jax.ShapeDtypeStruct((8, latent), F32),
         ],
         scratch_shapes=[
             pltpu.VMEM((table.shape[0] + 8, LANES), F32),
             pltpu.VMEM((2 * peers * owned, latent), BF16),
+            pltpu.VMEM((8, latent), F32),
         ],
         compiler_params=pltpu.CompilerParams(vmem_limit_bytes=60 * MIB),
         cost_estimate=pl.CostEstimate(
@@ -452,6 +461,7 @@
         edge_out,
         gain_e,
         shift_e,
+        coarse,
         node_in,
         node_out,
         gain_n,
@@ -460,13 +470,13 @@
 
     new_coarse = pl.pallas_call(
         coarse_kernel,
-        in_specs=[pl.BlockSpec(memory_space=pltpu.VMEM)] * 6,
+        in_specs=[pl.BlockSpec(memory_space=pltpu.VMEM)] * 7,
         out_specs=pl.BlockSpec(memory_space=pltpu.VMEM),
         out_shape=jax.ShapeDtypeStruct(coarse.shape, BF16),
-        scratch_shapes=[pltpu.VMEM(chunk, F32), pltpu.VMEM((8, 2 * latent), F32)],
+        scratch_shapes=[pltpu.VMEM(chunk, F32), pltpu.VMEM((8, latent), F32)],
         compiler_params=pltpu.CompilerParams(vmem_limit_bytes=16 * MIB),
         name="coarse_nodes",
-    )(parts, coarse, node_in, node_out, gain_n, shift_n)
+    )(parts, coarse, begun, node_in, node_out, gain_n, shift_n)
     return (new_nodes, new_coarse, new_edges)
 
 

time: 65.5 us -> 66.2 us (1.011)
  local copies, waits for them, and re-layouts: 1.48 us -> 2.19 us
    unnamed x24 -> x26, local copies, waits for them, and re-layouts: 0.06 us -> 0.77 us
where the time goes in v1:
time: 66.2 us; the launch traced here: 65.9 us
  starting transfers between devices  26.8 us (40%)
  Pallas kernels  21.7 us (33%)
  waiting for transfers between devices  11.4 us (17%)
  local copies, waits for them, and re-layouts  2.19 us (3%)
  blocking collectives  2.17 us (3%)
  between operations  0.83 us (1%)
  other arithmetic  0.79 us (1%)
    all_to_all x1, starting transfers between devices, on_device(): table = lax.all_to_all(copies, ('region', 'pair'), 0, 0, tiled=True)  15 us
    pallas_call x1, Pallas kernels, on_device(): pl.pallas_call(fine_edge_kernel, grid=(blocks,), in_specs=[smem, smem, wh...  11.3 us
    all_to_all x1, starting transfers between devices, on_device(): lax.all_to_all(chip_sum.reshape((peers,) + chunk), ('region', 'pair'), 0,...  7.09 us
    all_to_all x1, waiting for transfers between devices, on_device(): table = lax.all_to_all(copies, ('region', 'pair'), 0, 0, tiled=True)  6.49 us
    pallas_call x1, Pallas kernels, coarse_edges(): pl.pallas_call(coarse_edge_kernel, in_specs=[smem, vmem, vmem, anywhere,...  5.63 us
    pallas_call x1, Pallas kernels, on_device(): pl.pallas_call(functools.partial(local_kernel, peers=peers), grid=(blocks...  3.56 us
    all_to_all x1, waiting for transfers between devices, on_device(): lax.all_to_all(chip_sum.reshape((peers,) + chunk), ('region', 'pair'), 0,...  3.49 us
    ppermute x1, starting transfers between devices, on_device(): low = lax.ppermute(nodes, 'region', forward)  3.08 us
  transfers between devices with their start and end apart: 5, of which 3 were waited for; matrix products, arithmetic and copies ran while one was open for 0% of the time, Pallas kernels for 31%

profile of v1, /device:TPU:32, one launch (start us, length us, event | category | flops | bytes accessed | tf_op | source)
XLA Modules:
  0.0 65.9 jit_solution(15258803712919318602)
XLA Ops:
  0.6 1.4 %broadcast_in_dim.8 = bf16[128,8,128]{2,1,0:T(8,128)(2,1)} broadcast(bf16[8,128]{1,0:T(8,128)(2,1)} %bitcast.14), dimensions={1,2} | broadcast | bytes 264192 | tf_op jit(solution)/shard_map/broadcast_in_dim | solution.py:357
  2.0 15.0 %all-to-all-start = ((bf16[128,8,128]{2,1,0:T(8,128)(2,1)}), bf16[128,8,128]{2,1,0:T(8,128)(2,1)S(1)}, u32[]{:S(2)}, u32[]{:S(2)}) async-start(bf16[128,8,128]{2,1,0:T(8,128)(2,1)} %broadcast_in_dim.8), calls=%async_computation | async-start | bytes 524288 | tf_op jit(solution)/shard_map/all_to_all | solution.py:358
  17.1 3.1 %collective-permute-start = (bf16[256,512]{1,0:T(8,128)(2,1)}, bf16[256,512]{1,0:T(8,128)(2,1)S(1)}, u32[]{:S(2)}, u32[]{:S(2)}) collective-permute-start(bf16[256,512]{1,0:T(8,128)(2,1)} %nodes_ref.3), channel_id=1, source_target_pairs={{0,16},{16,32},{32,48},{48,64},{64,80},{80,96},{96,112},{112,128},... | collective-permute-start | bytes 786440 | tf_op jit(solution)/shard_map/ppermute | solution.py:362
  20.1 1.4 %collective-permute-start.1 = (bf16[256,512]{1,0:T(8,128)(2,1)}, bf16[256,512]{1,0:T(8,128)(2,1)S(1)}, u32[]{:S(2)}, u32[]{:S(2)}) collective-permute-start(bf16[256,512]{1,0:T(8,128)(2,1)} %nodes_ref.3), channel_id=1, source_target_pairs={{16,0},{32,16},{48,32},{64,48},{80,64},{96,80},{112,96},{128,112},... | collective-permute-start | bytes 786440 | tf_op jit(solution)/shard_map/ppermute | solution.py:363
  21.6 3.6 %local.1 = (bf16[1536,512]{1,0:T(8,128)(2,1)S(1)}, s32[12,128]{1,0:T(8,128)S(1)}) custom-call(s32[1]{0:T(128)} %bitcast.core_ref, s32[2]{0:T(128)} %counts_ref.3, s32[12,128]{1,0:T(8,128)} %bitcast.24, s32[12,128]{1,0:T(8,128)} %bitcast.26, bf16[1536,512]{1,0:T(8,128)(2,1)} %edges_ref.5, bf16[256,512]{1,0:T(8,128)(2,1)} %nodes_ref.3, ...), custom_call_target="tpu_custom_call" | custom-call | flops 1811939328 | bytes 6291456 | tf_op jit(solution)/shard_map/local/pallas_call | solution.py:374
  25.1 0.0 copy-start.1
  25.2 0.0 copy-start.5
  25.2 6.5 %all-to-all-done = bf16[128,8,128]{2,1,0:T(8,128)(2,1)S(1)} async-done(((bf16[128,8,128]{2,1,0:T(8,128)(2,1)}), bf16[128,8,128]{2,1,0:T(8,128)(2,1)S(1)}, u32[]{:S(2)}, u32[]{:S(2)}) %all-to-all-start) | async-done | bytes 262176 | tf_op jit(solution)/shard_map/all_to_all | solution.py:358
  31.7 2.2 %all_gather.3.table_ref = bf16[2048,128]{1,0:T(8,128)(2,1)S(1)} all-gather(bf16[1024,128]{1,0:T(8,128)(2,1)S(1)} %bitcast.23), channel_id=1, replica_groups=mesh['region'=16,'pair'=8,'core'=2] {'core'}, dimensions={0}, use_global_device_ids=true | all-gather | bytes 786432 | tf_op jit(solution)/shard_map/all_gather | solution.py:393
  33.8 0.0 copy-done.7
  33.8 0.0 copy-done.8
  33.8 5.6 %coarse_edges.1 = (bf16[1024,128]{1,0:T(8,128)(2,1)S(1)}, bf16[1024,128]{1,0:T(8,128)(2,1)S(1)}) custom-call(s32[1]{0:T(128)} %bitcast.core_ref, s32[12,128]{1,0:T(8,128)S(1)} %get-tuple-element.17.places.places_ref, bf16[1536,512]{1,0:T(8,128)(2,1)S(1)} %get-tuple-element.24.before_ref, bf16[1536,512]{1,0:T(8,128)(2,1)} %edges_ref.5, ...), custom_call_target="tpu_custom_call" | custom-call | tf_op jit(solution)/shard_map/coarse_edges/pallas_call | solution.py:305
  39.5 0.0 copy-done.1
  39.5 0.0 copy-done.5
  39.5 0.0 copy-done
  39.5 0.0 collective-permute-done.low_ref
  39.5 0.0 collective-permute-done.1.high_ref
  39.5 0.0 copy-start.12
  39.5 0.2 collective-permute-start.2
  39.8 1.4 %collective-permute-done.2 = bf16[1024,128]{1,0:T(8,128)(2,1)S(1)} collective-permute-done((bf16[1024,128]{1,0:T(8,128)(2,1)S(1)}, bf16[1024,128]{1,0:T(8,128)(2,1)S(1)}, u32[]{:S(2)}, u32[]{:S(2)}) %collective-permute-start.2) | collective-permute-done | bytes 262176 | tf_op jit(solution)/shard_map/ppermute | solution.py:398
  41.2 0.8 %add_convert_fusion = bf16[1024,128]{1,0:T(8,128)(2,1)} fusion(bf16[1024,128]{1,0:T(8,128)(2,1)S(1)} %collective-permute-done.2, bf16[1024,128]{1,0:T(8,128)(2,1)S(1)} %get-tuple-element.21), kind=kLoop, calls=%fused_computation | loop fusion | flops 524288 | bytes 786432 | tf_op jit(solution)/shard_map/convert_element_type | solution.py:399
  42.0 7.1 %all-to-all-start.1 = ((bf16[128,8,128]{2,1,0:T(8,128)(2,1)}), bf16[128,8,128]{2,1,0:T(8,128)(2,1)S(1)}, u32[]{:S(2)}, u32[]{:S(2)}) async-start(bf16[128,8,128]{2,1,0:T(8,128)(2,1)} %bitcast.11), calls=%async_computation.1 | async-start | bytes 524288 | tf_op jit(solution)/shard_map/all_to_all | solution.py:401
  49.1 0.0 copy-start.2
  49.1 0.0 copy-start.3
  49.1 0.0 copy-start.6
  49.1 0.0 copy-start.9
  49.1 0.0 copy-start.10
  49.1 11.3 %fine_edges.1 = (bf16[1536,512]{1,0:T(8,128)(2,1)}, bf16[256,512]{1,0:T(8,128)(2,1)}, f32[8,512]{1,0:T(8,128)}) custom-call(s32[1]{0:T(128)} %bitcast.core_ref, s32[2]{0:T(128)} %counts_ref.3, s32[12,128]{1,0:T(8,128)} %copy-done.5, s32[12,128]{1,0:T(8,128)} %bitcast.25, s32[12,128]{1,0:T(8,128)} %bitcast.27, bf16[1536,512]{1,0:T(8,128)(2,1)} %copy-done.1, ...), custom_call_target="tpu_custom_call" | custom-call | flops 3623878656 | bytes 10485760 | tf_op jit(solution)/shard_map/fine_edges/pallas_call | solution.py:405
  60.4 3.5 %all-to-all-done.1.parts_ref = bf16[128,8,128]{2,1,0:T(8,128)(2,1)S(1)} async-done(((bf16[128,8,128]{2,1,0:T(8,128)(2,1)}), bf16[128,8,128]{2,1,0:T(8,128)(2,1)S(1)}, u32[]{:S(2)}, u32[]{:S(2)}) %all-to-all-start.1) | async-done | bytes 262176 | tf_op jit(solution)/shard_map/all_to_all | solution.py:401
  63.9 0.0 copy-done.3
  64.0 0.7 %copy-done.4 = f32[8,512]{1,0:T(8,128)S(1)} copy-done((f32[8,512]{1,0:T(8,128)S(1)}, f32[8,512]{1,0:T(8,128)}, u32[]{:S(2)}) %copy-start.4) | copy-done | bytes 16408
  64.7 1.2 %coarse_nodes.1 = bf16[2,512]{1,0:T(2,128)(2,1)} custom-call(bf16[128,8,128]{2,1,0:T(8,128)(2,1)S(1)} %all-to-all-done.1.parts_ref, bf16[2,512]{1,0:T(2,128)(2,1)S(1)} %copy-done.6, f32[8,512]{1,0:T(8,128)S(1)} %copy-done.4, bf16[1024,512]{1,0:T(8,128)(2,1)S(1)} %copy-done.2, bf16[512,512]{1,0:T(8,128)(2,1)S(1)} %copy-done.3, f32[1,512]{1,0:T(1,128)S(1)} %bitcast.20, ...), custom_call_target="tpu_custom_call" | custom-call | tf_op jit(solution)/shard_map/coarse_nodes/pallas_call | solution.py:471
  (11 shorter events, 0.0 us)
Async XLA Ops:
  2.0 29.6 %all-to-all-start = ((bf16[128,8,128]{2,1,0:T(8,128)(2,1)}), bf16[128,8,128]{2,1,0:T(8,128)(2,1)S(1)}, u32[]{:S(2)}, u32[]{:S(2)}) async-start(bf16[128,8,128]{2,1,0:T(8,128)(2,1)} %broadcast_in_dim.8), calls=%async_computation | async-start | bytes 524288 | tf_op jit(solution)/shard_map/all_to_all | solution.py:358
  17.1 22.4 %collective-permute-start = (bf16[256,512]{1,0:T(8,128)(2,1)}, bf16[256,512]{1,0:T(8,128)(2,1)S(1)}, u32[]{:S(2)}, u32[]{:S(2)}) collective-permute-start(bf16[256,512]{1,0:T(8,128)(2,1)} %nodes_ref.3), channel_id=1, source_target_pairs={{0,16},{16,32},{32,48},{48,64},{64,80},{80,96},{96,112},{112,128},... | collective-permute-start | bytes 786440 | tf_op jit(solution)/shard_map/ppermute | solution.py:362
  20.1 19.4 %collective-permute-start.1 = (bf16[256,512]{1,0:T(8,128)(2,1)}, bf16[256,512]{1,0:T(8,128)(2,1)S(1)}, u32[]{:S(2)}, u32[]{:S(2)}) collective-permute-start(bf16[256,512]{1,0:T(8,128)(2,1)} %nodes_ref.3), channel_id=1, source_target_pairs={{16,0},{32,16},{48,32},{64,48},{80,64},{96,80},{112,96},{128,112},... | collective-permute-start | bytes 786440 | tf_op jit(solution)/shard_map/ppermute | solution.py:363
  21.6 12.3 %copy-start.7 = (f32[512]{0:T(512)S(1)}, f32[512]{0:T(512)}, u32[]{:S(2)}) copy-start(f32[512]{0:T(512)} %param.22) | copy-start | bytes 6148
  21.6 12.3 %copy-start.8 = (f32[512]{0:T(512)S(1)}, f32[512]{0:T(512)}, u32[]{:S(2)}) copy-start(f32[512]{0:T(512)} %param.23) | copy-start | bytes 6148
  25.1 14.3 %copy-start.1 = (bf16[1536,512]{1,0:T(8,128)(2,1)}, bf16[1536,512]{1,0:T(8,128)(2,1)S(1)}, u32[]{:S(2)}) copy-start(bf16[1536,512]{1,0:T(8,128)(2,1)S(1)} %get-tuple-element.24.before_ref) | copy-start | bytes 4718596
  25.2 14.3 %copy-start.5 = (s32[12,128]{1,0:T(8,128)}, s32[12,128]{1,0:T(8,128)S(1)}, u32[]{:S(2)}) copy-start(s32[12,128]{1,0:T(8,128)S(1)} %get-tuple-element.17.places.places_ref) | copy-start | bytes 18436
  33.8 5.7 %copy-start = (bf16[2048,128]{1,0:T(8,128)(2,1)}, bf16[2048,128]{1,0:T(8,128)(2,1)S(1)}, u32[]{:S(2)}) copy-start(bf16[2048,128]{1,0:T(8,128)(2,1)S(1)} %all_gather.3.table_ref) | copy-start | bytes 1572868
  39.5 9.6 %copy-start.11 = (bf16[256,512]{1,0:T(8,128)(2,1)}, bf16[256,512]{1,0:T(8,128)(2,1)S(1)}, u32[]{:S(2)}) copy-start(bf16[256,512]{1,0:T(8,128)(2,1)S(1)} %collective-permute-done.low_ref) | copy-start | bytes 786436
  39.5 9.5 %copy-start.12 = (bf16[256,512]{1,0:T(8,128)(2,1)}, bf16[256,512]{1,0:T(8,128)(2,1)S(1)}, u32[]{:S(2)}) copy-start(bf16[256,512]{1,0:T(8,128)(2,1)S(1)} %collective-permute-done.1.high_ref) | copy-start | bytes 786436
  39.5 1.6 %collective-permute-start.2 = (bf16[1024,128]{1,0:T(8,128)(2,1)S(1)}, bf16[1024,128]{1,0:T(8,128)(2,1)S(1)}, u32[]{:S(2)}, u32[]{:S(2)}) collective-permute-start(bf16[1024,128]{1,0:T(8,128)(2,1)S(1)} %get-tuple-element.23), channel_id=1, source_target_pairs={{0,1},{1,0},{2,3},{3,2},{4,5},{5,4},{6,7},{7,6},{8,9},{9,8},{10,11... | collective-permute-start | bytes 786440 | tf_op jit(solution)/shard_map/ppermute | solution.py:398
  42.0 21.9 %all-to-all-start.1 = ((bf16[128,8,128]{2,1,0:T(8,128)(2,1)}), bf16[128,8,128]{2,1,0:T(8,128)(2,1)S(1)}, u32[]{:S(2)}, u32[]{:S(2)}) async-start(bf16[128,8,128]{2,1,0:T(8,128)(2,1)} %bitcast.11), calls=%async_computation.1 | async-start | bytes 524288 | tf_op jit(solution)/shard_map/all_to_all | solution.py:401
  49.1 14.8 %copy-start.2 = (bf16[1024,512]{1,0:T(8,128)(2,1)S(1)}, bf16[1024,512]{1,0:T(8,128)(2,1)}, u32[]{:S(2)}) copy-start(bf16[1024,512]{1,0:T(8,128)(2,1)} %w_in_ref.3) | copy-start | bytes 3145732
  49.1 14.8 %copy-start.3 = (bf16[512,512]{1,0:T(8,128)(2,1)S(1)}, bf16[512,512]{1,0:T(8,128)(2,1)}, u32[]{:S(2)}) copy-start(bf16[512,512]{1,0:T(8,128)(2,1)} %w_out_ref.5) | copy-start | bytes 1572868
  49.1 14.8 %copy-start.6 = (bf16[2,512]{1,0:T(2,128)(2,1)S(1)}, bf16[2,512]{1,0:T(2,128)(2,1)}, u32[]{:S(2)}) copy-start(bf16[2,512]{1,0:T(2,128)(2,1)} %coarse_ref.3) | copy-start | bytes 6148
  49.1 14.8 %copy-start.9 = (f32[512]{0:T(512)S(1)}, f32[512]{0:T(512)}, u32[]{:S(2)}) copy-start(f32[512]{0:T(512)} %param.26) | copy-start | bytes 6148
  49.1 14.8 %copy-start.10 = (f32[512]{0:T(512)S(1)}, f32[512]{0:T(512)}, u32[]{:S(2)}) copy-start(f32[512]{0:T(512)} %param.27) | copy-start | bytes 6148
  63.9 0.7 %copy-start.4 = (f32[8,512]{1,0:T(8,128)S(1)}, f32[8,512]{1,0:T(8,128)}, u32[]{:S(2)}) copy-start(f32[8,512]{1,0:T(8,128)} %get-tuple-element.29.begun_ref) | copy-start | bytes 49156
